TPU v7x, 128 devices: a whole 4x4x4 slice. The times are simulated.
128 devices in a mesh: shot: 4 (over z), slab: 32 (over y, x, core).
Axes of the slice: x: 4, y: 4, z: 4, core: 2. Of those that a mesh axis runs over, the one named last changes fastest.
Arguments:
- courant: float32 [4, 256, 256, 256], P('shot', 'slab'), may hold values from 0.05 to 0.3
- adj_prev: float32 [4, 256, 256, 256], P('shot', 'slab'), may hold values from -6 to 6
- adj_cur: float32 [4, 256, 256, 256], P('shot', 'slab'), may hold values from -6 to 6
- accel: float32 [4, 3, 256, 256, 256], P('shot', None, 'slab'), may hold values from -6 to 6
- res_data: float32 [4, 3, 512], P('shot'), may hold values from -6 to 6
- rec_index: int32 [4, 512], P('shot'), may hold values from 0 to 16777215
- intersection: int32 [4, 8], P('shot'), may hold values from 0 to 15, as said below
- model: float32 [256, 512, 256], P('slab', 'shot'), may hold values from 0.5 to 2
Outputs:
- new_model: float32 [256, 512, 256], P('slab', 'shot')
- adj_state: float32 [4, 256, 256, 256], P('shot', 'slab')
- born_field: float32 [4, 256, 256, 256], P('shot', 'slab')
Inputs may be any that keep to these rules, and one draw needn't show every extreme that they name: `intersection`: each shot's ids are 8 consecutive tiles; some shot starts at 0 and some shot ends at 15.
All inputs are finite; a program needn't handle non-finite values.
Results may differ from a plain program's by a relative error of at most 0.00012.
Values sent between devices are 32-bit elements; how exact they have to be, the bound alone decides.
A program may use at most 128 MiB of HBM per device.

v0:
```python
import jax
import jax.numpy as jnp
from jax import lax
from jax.sharding import PartitionSpec as P


def extended(x, sides, width):
    for axis, dim in sides:
        devices, length = (lax.axis_size(axis), x.shape[dim])
        up = [(i, (i + 1) % devices) for i in range(devices - 1)]
        down = [(j, i) for i, j in up]
        last = lax.slice_in_dim(x, length - width, length, axis=dim)
        leading = lax.slice_in_dim(x, 0, width, axis=dim)
        before = lax.ppermute(last, axis, up)
        after = lax.ppermute(leading, axis, down)
        x = jnp.concatenate([before, x, after], axis=dim)
    return x


def lap_inner(ext):
    center = ext[1:-1]
    side = jnp.pad(center, ((0, 0), (1, 1), (1, 1)))
    nbrs = (
        ext[:-2]
        + ext[2:]
        + side[:, :-2, 1:-1]
        + side[:, 2:, 1:-1]
        + side[:, 1:-1, :-2]
        + side[:, 1:-1, 2:]
    )
    return nbrs - 6.0 * center


def wave_step(ext, before, coeff):
    return 2.0 * ext[1:-1] - before + coeff * lap_inner(ext)


def local_cells(field, receivers, first_plane):
    plane_cells = field.shape[1] * field.shape[2]
    where = receivers - first_plane * plane_cells
    inside = (where >= 0) & (where < field.shape[0] * plane_cells)
    return (jnp.where(inside, where, 0), inside)


def inject(field, receivers, values, first_plane):
    where, inside = local_cells(field, receivers, first_plane)
    shape = field.shape
    return field.reshape(-1).at[where].add(jnp.where(inside, values, 0.0)).reshape(shape)


def sample(field, receivers, first_plane):
    where, inside = local_cells(field, receivers, first_plane)
    return jnp.where(inside, field.reshape(-1)[where], 0.0)


def local(courant, adj_prev, adj_cur, accel, res_data, rec_index, intersection, model):
    coeff = courant[0]
    before = adj_prev[0]
    now = adj_cur[0]
    forward = accel[0]
    residual = res_data[0]
    receivers = rec_index[0]
    tile_ids = intersection[0]
    depth, wide_x, wide_y = coeff.shape
    first_plane = lax.axis_index("slab") * depth
    image = jnp.zeros((depth, wide_x, wide_y), jnp.float32)
    for turn in range(2):
        ext = extended(now, (("slab", 0),), 1)
        later = inject(wave_step(ext, before, coeff), receivers, residual[2 - turn], first_plane)
        image = image + forward[1 - turn] * later
        before, now = (now, later)
    tiles = tile_ids.shape[0]
    tile_x = wide_x // tiles
    shots = lax.axis_size("shot")
    owned_tiles = model.shape[1] // tile_x
    total_tiles = owned_tiles * shots
    onehot = (jnp.arange(total_tiles)[:, None] == tile_ids[None, :]).astype(jnp.float32)
    spread = jnp.einsum(
        "mj,zjxy->zmxy",
        onehot,
        image.reshape(depth, tiles, tile_x, wide_y),
        precision=lax.Precision.HIGHEST,
    )
    outbox = spread.reshape(depth, shots, owned_tiles * tile_x, wide_y)
    inbox = lax.all_to_all(outbox, "shot", split_axis=1, concat_axis=1, tiled=True)
    owned = jnp.sum(inbox, axis=1)
    whole = lax.all_gather(owned, "shot", axis=1, tiled=True)
    gap = jnp.einsum(
        "mj,zmxy->zjxy",
        onehot,
        whole.reshape(depth, total_tiles, tile_x, wide_y),
        precision=lax.Precision.HIGHEST,
    )
    weight = coeff * gap.reshape(depth, wide_x, wide_y)
    born_now = weight * forward[0]
    born_before = jnp.zeros((depth, wide_x, wide_y), jnp.float32)
    trace = sample(born_now, receivers, first_plane)
    num = jnp.sum(residual[0] * trace)
    den = jnp.sum(trace * trace)
    for tick in range(1, 3):
        ext = extended(born_now, (("slab", 0),), 1)
        born_later = wave_step(ext, born_before, coeff) + weight * forward[tick]
        trace = sample(born_later, receivers, first_plane)
        num = num + jnp.sum(residual[tick] * trace)
        den = den + jnp.sum(trace * trace)
        born_before, born_now = (born_now, born_later)
    num_all, den_all = lax.psum((num, den), ("shot", "slab"))
    alpha = num_all / (den_all + 1e-06)
    new_model = model - alpha * owned
    return (new_model, now[None], born_now[None])


def solution(mesh):
    in_specs = (
        P("shot", "slab", None, None),
        P("shot", "slab", None, None),
        P("shot", "slab", None, None),
        P("shot", None, "slab", None, None),
        P("shot", None, None),
        P("shot", None),
        P("shot", None),
        P("slab", "shot", None),
    )
    out_specs = (
        P("slab", "shot", None),
        P("shot", "slab", None, None),
        P("shot", "slab", None, None),
    )
    return jax.shard_map(local, mesh=mesh, in_specs=in_specs, out_specs=out_specs, check_vma=False)
```

profile of v0, /device:TPU:0, one launch (start us, length us, event | category | flops | bytes accessed | tf_op | source)
XLA Modules:
  0.0 378.8 jit_solution(4352774802263474346)
XLA Ops:
  13.0 1.8 collective-permute-done.1
  14.8 9.2 %fusion.8 = f32[8,256,256]{2,1,0:T(8,128)S(1)} fusion(f32[8,256,256]{2,1,0:T(8,128)} %bitcast.90, f32[1,256,256]{2,1,0:T(8,128)S(1)} %collective-permute-done.1, f32[1,256,256]{2,1,0:T(8,128)S(1)} %collective-permute-done, f32[1,8,256,256]{3,2,1,0:T(8,128)} %param.8, f32[1,8,256,256]{3,2,1,0:T(8,128)} %param.9), kind=kLoop, calls=%fused_computation.30 | loop fusion | flops 6815744 | bytes 8912896 | tf_op jit(solution)/shard_map/add | solution.py:35
  25.1 4.8 %scatter_fusion = f32[524288]{0:T(1024)S(1)} fusion(f32[524288]{0:T(1024)S(1)} %bitcast.84, s32[512]{0:T(512)S(1)} %bitcast.102, f32[512]{0:T(512)S(1)} %get-tuple-element.29), kind=kCustom, calls=%fused_computation.3 | custom fusion | flops 512 | bytes 8192 | tf_op jit(solution)/shard_map/scatter-add | solution.py:48
  30.1 6.6 %collective-permute-start.2 = (f32[1,256,256]{2,1,0:T(8,128)S(1)}, f32[1,256,256]{2,1,0:T(8,128)S(1)}, u32[]{:S(2)}, u32[]{:S(2)}) collective-permute-start(f32[1,256,256]{2,1,0:T(8,128)S(1)} %slice.175), channel_id=1, source_target_pairs={{0,1},{1,2},{2,3},{3,4},{4,5},{5,6},{6,7},{7,8},{8,9},{9,10},{10,1... | collective-permute-start | bytes 786440 | tf_op jit(solution)/shard_map/ppermute | solution.py:14
  38.1 4.6 %fusion.45 = (f32[1,1,8,256,256]{4,3,2,1,0:T(8,128)}, f32[1,1,8,256,256]{4,3,2,1,0:T(8,128)}) fusion(f32[1,3,8,256,256]{4,3,2,1,0:T(8,128)} %param.11), kind=kLoop, calls=%fused_computation.94 | loop fusion | bytes 8388608 | tf_op jit(solution)/shard_map/slice | solution.py:70
  42.7 1.6 reshape.120
  44.3 3.0 reshape.119
  47.4 8.3 %fusion.15 = f32[8,256,256]{2,1,0:T(8,128)S(1)} fusion(f32[8,256,256]{2,1,0:T(8,128)} %reshape.120, f32[1,256,256]{2,1,0:T(8,128)S(1)} %collective-permute-done.3, f32[1,256,256]{2,1,0:T(8,128)S(1)} %collective-permute-done.2, f32[1,8,256,256]{3,2,1,0:T(8,128)S(1)} %copy-done, f32[1,8,256,256]{3,2,1,0:T(8,128)} %param.10), kind=kLoop, calls=%fused_computation.37 | loop fusion | flops 6815744 | bytes 8912896 | tf_op jit(solution)/shard_map/add | solution.py:35
  55.7 2.4 copy.27
  58.1 6.9 %scatter_fusion.1 = f32[524288]{0:T(1024)} fusion(f32[524288]{0:T(1024)} %bitcast.85, s32[512]{0:T(512)S(1)} %bitcast.103, f32[512]{0:T(512)S(1)} %get-tuple-element.28), kind=kCustom, calls=%fused_computation.4 | custom fusion | flops 512 | bytes 8192 | tf_op jit(solution)/shard_map/scatter-add | solution.py:48
  65.0 2.8 reshape.122
  67.8 4.4 %multiply_add_fusion = f32[8,8,32,256]{3,2,1,0:T(8,128)S(1)} fusion(f32[8,8,32,256]{3,2,1,0:T(8,128)} %bitcast.87, f32[8,8,32,256]{3,2,1,0:T(8,128)} %reshape.122, f32[8,8,32,256]{3,2,1,0:T(8,128)} %bitcast.95, f32[8,8,32,256]{3,2,1,0:T(8,128)} %reshape.119), kind=kLoop, calls=%fused_computation.73 | loop fusion | flops 1572864 | bytes 10485760 | tf_op jit(solution)/shard_map/add | solution.py:70
  72.3 2.8 convolution_bitcast_fusion
  75.1 2.4 copy.19
  77.9 55.2 %all_to_all.5 = f32[8,4,128,256]{3,2,0,1:T(8,128)} all-to-all(f32[8,4,128,256]{3,2,0,1:T(8,128)S(1)} %copy.20), channel_id=1, replica_groups=mesh['shot'=4,'slab'=32] {'shot'}, dimensions={1} | all-to-all | bytes 8388608 | tf_op jit(solution)/shard_map/all_to_all | solution.py:85
  133.2 3.6 reduce_sum.63
  136.8 49.9 %all-gather.2.cloned.1.call-done = f32[8,512,256]{2,1,0:T(8,128)} async-done(((f32[8,128,256]{2,1,0:T(8,128)}), f32[8,512,256]{2,1,0:T(8,128)}) %all-gather.2.cloned.1.call-update) | async-done | bytes 4194320 | tf_op jit(solution)/shard_map/all_gather | solution.py:87
  186.6 6.0 %fusion.37 = f32[8,8,32,256]{3,1,2,0:T(8,128)S(1)} fusion(f32[8,16,32,256]{3,2,1,0:T(8,128)} %bitcast.101, s32[8]{0:T(128)S(1)} %bitcast.111), kind=kOutput, calls=%fused_computation.74 | convolution fusion | flops 100663424 | bytes 6291488 | tf_op jit(solution)/shard_map/mj,zmxy->zjxy/dot_general | solution.py:88
  193.3 2.9 bitcast_multiply_fusion.2
  196.3 1.7 collective-permute-start.4
  202.7 3.6 fusion.23
  207.7 6.7 %collective-permute-start.6 = (f32[1,256,256]{2,1,0:T(8,128)S(1)}, f32[1,256,256]{2,1,0:T(8,128)S(1)}, u32[]{:S(2)}, u32[]{:S(2)}) collective-permute-start(f32[1,256,256]{2,1,0:T(8,128)S(1)} %get-tuple-element.17), channel_id=1, source_target_pairs={{0,1},{1,2},{2,3},{3,4},{4,5},{5,6},{6,7},{7,8},{8,9},{9,10},{10,1... | collective-permute-start | bytes 786440 | tf_op jit(solution)/shard_map/ppermute | solution.py:14
  215.9 1.6 multiply_multiply_fusion
  217.5 20.5 %gather_fusion = f32[512]{0:T(512)S(1)} fusion(f32[524288]{0:T(1024)} %multiply_multiply_fusion, s32[1024]{0:T(1024)S(1)} %pad_clamp_fusion), kind=kCustom, calls=%fused_computation | custom fusion | bytes 6144 | tf_op jit(solution)/shard_map/gather | solution.py:53
  238.1 4.0 %copy.30 = f32[256,2,8,128]{3,1,2,0:T(2,128)} copy(f32[256,2,8,128]{3,2,1,0:T(8,128)} %bitcast.86) | data formatting | bytes 4194304
  242.1 20.5 %gather_fusion.1 = f32[512]{0:T(512)S(1)} fusion(f32[524288]{0:T(1024)} %bitcast.97, s32[1024]{0:T(1024)S(1)} %pad_clamp_fusion), kind=kCustom, calls=%fused_computation.1 | custom fusion | bytes 6144 | tf_op jit(solution)/shard_map/gather | solution.py:53
  262.6 9.2 %fusion.31 = f32[8,256,256]{2,1,0:T(8,128)S(1)} fusion(f32[8,256,256]{2,1,0:T(8,128)} %copy-done.4, f32[1,256,256]{2,1,0:T(8,128)S(1)} %collective-permute-done.7, f32[1,256,256]{2,1,0:T(8,128)S(1)} %collective-permute-done.6, f32[1,8,256,256]{3,2,1,0:T(8,128)S(1)} %copy-done, f32[1,3,8,256,256]{4,3,2,1,0:T(8,128)} %param.11, f32[8,8,32,256]{3,2,1,0:T(8,128)} %copy-done.1), kind=kLoop, calls=%fused_computation.53 | loop fusion | flops 8912896 | bytes 13107200 | tf_op jit(solution)/shard_map/add | solution.py:102
  271.9 2.4 copy.31
  274.3 20.5 %gather_fusion.2 = f32[512]{0:T(512)S(1)} fusion(f32[524288]{0:T(1024)} %bitcast.96, s32[1024]{0:T(1024)S(1)} %pad_clamp_fusion), kind=kCustom, calls=%fused_computation.2 | custom fusion | bytes 6144 | tf_op jit(solution)/shard_map/gather | solution.py:53
  299.3 1.6 broadcast_in_dim_reshape.3
  300.9 67.4 %all-reduce.4 = (f32[]{:T(128)}, f32[]{:T(128)}) all-reduce(f32[]{:T(128)S(6)} %add.156, f32[]{:T(128)S(6)} %add.158), channel_id=1, replica_groups=mesh['shot'=4,'slab'=32] {'shot','slab'}, use_global_device_ids=true, to_apply=%region_6.7 | all-reduce | flops 2 | bytes 16 | tf_op jit(solution)/shard_map/psum | solution.py:107
  369.7 2.3 multiply_subtract_fusion
  (50 shorter events, 17.8 us)
Async XLA Ops:
  7.2 179.5 %all-gather.2.cloned.1.call-start = ((), (), s32[]{:S(2)}) async-start(), calls=%async_computation.1 | async-start | bytes 5242880 | tf_op jit(solution)/shard_map/all_gather | solution.py:87
  8.3 4.7 %collective-permute-start = (f32[1,256,256]{2,1,0:T(8,128)S(1)}, f32[1,256,256]{2,1,0:T(8,128)S(1)}, u32[]{:S(2)}, u32[]{:S(2)}) collective-permute-start(f32[1,256,256]{2,1,0:T(8,128)S(1)} %get-tuple-element.23), channel_id=1, source_target_pairs={{0,1},{1,2},{2,3},{3,4},{4,5},{5,6},{6,7},{7,8},{8,9},{9,10},{10,1... | collective-permute-start | bytes 786440 | tf_op jit(solution)/shard_map/ppermute | solution.py:14
  9.6 5.2 %collective-permute-start.1 = (f32[1,256,256]{2,1,0:T(8,128)S(1)}, f32[1,256,256]{2,1,0:T(8,128)S(1)}, u32[]{:S(2)}, u32[]{:S(2)}) collective-permute-start(f32[1,256,256]{2,1,0:T(8,128)S(1)} %get-tuple-element.24), channel_id=1, source_target_pairs={{1,0},{2,1},{3,2},{4,3},{5,4},{6,5},{7,6},{8,7},{9,8},{10,9},{11,1... | collective-permute-start | bytes 786440 | tf_op jit(solution)/shard_map/ppermute | solution.py:15
  29.9 12.8 %copy-start.2 = (f32[524288]{0:T(1024)}, f32[524288]{0:T(1024)S(1)}, u32[]{:S(2)}) copy-start(f32[524288]{0:T(1024)S(1)} %scatter_fusion) | copy-start | bytes 6291460
  30.1 17.3 %collective-permute-start.2 = (f32[1,256,256]{2,1,0:T(8,128)S(1)}, f32[1,256,256]{2,1,0:T(8,128)S(1)}, u32[]{:S(2)}, u32[]{:S(2)}) collective-permute-start(f32[1,256,256]{2,1,0:T(8,128)S(1)} %slice.175), channel_id=1, source_target_pairs={{0,1},{1,2},{2,3},{3,4},{4,5},{5,6},{6,7},{7,8},{8,9},{9,10},{10,1... | collective-permute-start | bytes 786440 | tf_op jit(solution)/shard_map/ppermute | solution.py:14
  36.8 10.6 %collective-permute-start.3 = (f32[1,256,256]{2,1,0:T(8,128)S(1)}, f32[1,256,256]{2,1,0:T(8,128)S(1)}, u32[]{:S(2)}, u32[]{:S(2)}) collective-permute-start(f32[1,256,256]{2,1,0:T(8,128)S(1)} %slice.178), channel_id=1, source_target_pairs={{1,0},{2,1},{3,2},{4,3},{5,4},{6,5},{7,6},{8,7},{9,8},{10,9},{11,1... | collective-permute-start | bytes 786440 | tf_op jit(solution)/shard_map/ppermute | solution.py:15
  44.3 3.1 copy-start
  67.8 4.4 %copy-start.8 = (s32[1,8]{1,0:T(1,128)S(1)}, s32[1,8]{1,0:T(1,128)}, u32[]{:S(2)}) copy-start(s32[1,8]{1,0:T(1,128)} %param.14) | copy-start | bytes 100
  193.3 9.4 %copy-start.1 = (f32[8,8,32,256]{3,2,1,0:T(8,128)}, f32[8,8,32,256]{3,2,1,0:T(8,128)S(1)}, u32[]{:S(2)}) copy-start(f32[8,8,32,256]{3,2,1,0:T(8,128)S(1)} %copy.22) | copy-start | bytes 6291460
  193.3 6.0 %copy-start.5 = (f32[1,1,8,256,256]{4,3,2,1,0:T(8,128)S(1)}, f32[1,1,8,256,256]{4,3,2,1,0:T(8,128)}, u32[]{:S(2)}) copy-start(f32[1,1,8,256,256]{4,3,2,1,0:T(8,128)} %get-tuple-element.16) | copy-start | bytes 6291460
  196.3 6.3 %collective-permute-start.4 = (f32[1,256,256]{2,1,0:T(8,128)S(1)}, f32[1,256,256]{2,1,0:T(8,128)S(1)}, u32[]{:S(2)}, u32[]{:S(2)}) collective-permute-start(f32[1,256,256]{2,1,0:T(8,128)S(1)} %get-tuple-element.19), channel_id=1, source_target_pairs={{0,1},{1,2},{2,3},{3,4},{4,5},{5,6},{6,7},{7,8},{8,9},{9,10},{10,1... | collective-permute-start | bytes 786440 | tf_op jit(solution)/shard_map/ppermute | solution.py:14
  198.0 4.7 %collective-permute-start.5 = (f32[1,256,256]{2,1,0:T(8,128)S(1)}, f32[1,256,256]{2,1,0:T(8,128)S(1)}, u32[]{:S(2)}, u32[]{:S(2)}) collective-permute-start(f32[1,256,256]{2,1,0:T(8,128)S(1)} %get-tuple-element.20), channel_id=1, source_target_pairs={{1,0},{2,1},{3,2},{4,3},{5,4},{6,5},{7,6},{8,7},{9,8},{10,9},{11,1... | collective-permute-start | bytes 786440 | tf_op jit(solution)/shard_map/ppermute | solution.py:15
  206.3 1.3 copy-start.4
  207.7 54.9 %collective-permute-start.6 = (f32[1,256,256]{2,1,0:T(8,128)S(1)}, f32[1,256,256]{2,1,0:T(8,128)S(1)}, u32[]{:S(2)}, u32[]{:S(2)}) collective-permute-start(f32[1,256,256]{2,1,0:T(8,128)S(1)} %get-tuple-element.17), channel_id=1, source_target_pairs={{0,1},{1,2},{2,3},{3,4},{4,5},{5,6},{6,7},{7,8},{8,9},{9,10},{10,1... | collective-permute-start | bytes 786440 | tf_op jit(solution)/shard_map/ppermute | solution.py:14
  214.4 48.3 %collective-permute-start.7 = (f32[1,256,256]{2,1,0:T(8,128)S(1)}, f32[1,256,256]{2,1,0:T(8,128)S(1)}, u32[]{:S(2)}, u32[]{:S(2)}) collective-permute-start(f32[1,256,256]{2,1,0:T(8,128)S(1)} %get-tuple-element.18), channel_id=1, source_target_pairs={{1,0},{2,1},{3,2},{4,3},{5,4},{6,5},{7,6},{8,7},{9,8},{10,9},{11,1... | collective-permute-start | bytes 786440 | tf_op jit(solution)/shard_map/ppermute | solution.py:15
  271.9 2.4 copy-start.7
  274.3 25.0 %copy-start.3 = (f32[524288]{0:T(1024)S(1)}, f32[524288]{0:T(1024)}, u32[]{:S(2)}) copy-start(f32[524288]{0:T(1024)} %scatter_fusion.1) | copy-start | bytes 6291460
  299.3 70.4 %copy-start.6 = (f32[8,128,256]{2,1,0:T(8,128)S(1)}, f32[8,128,256]{2,1,0:T(8,128)}, u32[]{:S(2)}) copy-start(f32[8,128,256]{2,1,0:T(8,128)} %reduce_sum.63) | copy-start | bytes 3145732
Sparse Core Ops, SparseCore 0:
  136.9 49.7 all-gather.1
where the time goes:
time: 382 us; the launch traced here: 379 us
  blocking collectives  123 us (32%)
  local copies, waits for them, and re-layouts  95.3 us (25%)
  other arithmetic  59 us (15%)
  waiting for transfers between devices  51.8 us (14%)
  starting transfers between devices  21.8 us (6%)
  between operations  19.4 us (5%)
  matrix products  8.8 us (2%)
    psum x1, blocking collectives, local(): num_all, den_all = lax.psum((num, den), ('shot', 'slab'))  67.4 us
    gather x3, local copies, waits for them, and re-layouts, sample(): return jnp.where(inside, field.reshape(-1)[where], 0.0)  61.6 us
    all_to_all x1, blocking collectives, local(): lax.all_to_all(outbox, 'shot', split_axis=1, concat_axis=1, tiled=True)  55.2 us
    all_gather x1, waiting for transfers between devices, local(): whole = lax.all_gather(owned, 'shot', axis=1, tiled=True)  49.9 us
    add x2, other arithmetic, wave_step(): return 2.0 * ext[1:-1] - before + coeff * lap_inner(ext)  17.5 us
    ppermute x4, starting transfers between devices, extended(): before = lax.ppermute(last, axis, up)  16.3 us
    unnamed x25, local copies, waits for them, and re-layouts  14.5 us
    add x2, other arithmetic, local(): born_later = wave_step(ext, born_before, coeff) + weight * forward[tick]  12.8 us
  transfers between devices with their start and end apart: 9, of which 3 were waited for; matrix products, arithmetic and copies ran while one was open for 16% of the time, Pallas kernels for 0%

commit v1 on v0

v1 whole, which is shorter than its diff:
```python
import functools

import jax
import jax.numpy as jnp
from jax import lax
from jax.experimental import pallas as pl
from jax.experimental.pallas import tpu as pltpu
from jax.sharding import PartitionSpec as P

MESH = pl.DeviceIdType.MESH
ORDER = (1, 2, 0, 3, 7, 4, 6, 5)
FIRST = (0, 1, 6, 7)


def radices(count):
    out = []
    while count > 1:
        step = 4 if count % 4 == 0 and (out or count == 4) else 2
        out.append(step)
        count //= step
    return out


def kernel(
    dims,
    inter_ref, res_ref, rec_ref, courant, prev, cur, accel, model,
    nm_out, adj_out, born_out,
    ac, ach, co, ap, ax, mo, p1, p1h, ad, img, v1, s2, w2, part,
    qd, ct, b1, b1h, b2, b2h, b3, wt, exs, exr, own, nm, stv, ar,
    ld, outs, h_s, h_r, p_s, p_r, b_s, b_r, st_s, st_r, z1_s, z1_r, z2_s, z2_r, ex_s, ex_r, ar_s, ar_r,
):
    shots, slabs, depth, wide, width, tiles, tx, nrec = dims
    f32 = jnp.float32
    z = lax.axis_index("shot")
    k = lax.axis_index("slab")
    par = z % 2
    pair_a = z + 1 - 2 * par
    pair_b = shots - 1 - z
    up = (k + 1) % slabs
    down = (k + slabs - 1) % slabs

    phases = []
    stride = 1
    for n in radices(slabs):
        coord = (k // stride) % n
        base = k - coord * stride
        phases.append((n, coord, [(z, base + ((coord + d) % n) * stride) for d in range(1, n)]))
        stride *= n
    phases.append((shots, z, [((z + d) % shots, k) for d in range(1, shots)]))

    barrier = pltpu.get_barrier_semaphore()
    greet = [(z, up), (z, down)] + [dev for phase in phases for dev in phase[2]]
    for dev in greet:
        pl.semaphore_signal(barrier, inc=1, device_id=dev, device_id_type=MESH)

    def strip(j):
        return slice(j * tx, j * tx + tx)

    def load(src, dst, at):
        copies = [pltpu.make_async_copy(src.at[:, strip(j)], dst.at[j], ld.at[at, j]) for j in range(tiles)]
        for copy in copies:
            copy.start()
        return copies

    l_cur = load(cur.at[0], ac, 0)
    l_co = load(courant.at[0], co, 1)
    l_ap = load(prev.at[0], ap, 2)
    l_a1 = load(accel.at[0, 1], ax.at[1], 3)
    l_a0 = load(accel.at[0, 0], ax.at[0], 4)
    l_a2 = load(accel.at[0, 2], ax.at[2], 5)
    l_mo = pltpu.make_async_copy(model, mo, ld.at[6, 0])
    l_mo.start()

    def wait(copies):
        for copy in copies:
            copy.wait()

    def remote(src, dst, send, recv, dev):
        return pltpu.make_async_remote_copy(
            src_ref=src, dst_ref=dst, send_sem=send, recv_sem=recv, device_id=dev, device_id_type=MESH
        )

    start = inter_ref[0, 0]
    stv[0] = jnp.full(stv.shape[1:], start, jnp.int32)

    pl.semaphore_wait(barrier, len(greet))

    halos_c = []
    for j in range(tiles):
        halos_c.append(remote(cur.at[0, depth - 1, strip(j)], ach.at[0, j], h_s.at[0, j], h_r.at[0, j], (z, up)))
        halos_c.append(remote(cur.at[0, 0, strip(j)], ach.at[1, j], h_s.at[1, j], h_r.at[1, j], (z, down)))
    for copy in halos_c:
        copy.start()
    st_a = remote(stv.at[0], stv.at[1], st_s.at[0], st_r.at[0], (pair_a, k))
    st_b = remote(stv.at[0], stv.at[2], st_s.at[1], st_r.at[1], (pair_b, k))
    st_a.start()
    st_b.start()

    rec = rec_ref[...] - k * (depth * wide * width)
    inside = (rec >= 0) & (rec < depth * wide * width)
    line = rec // width
    down_at, along = line // wide, line % wide
    row = jnp.where(inside, (along // tx * depth + down_at) * tx + along % tx, -1)
    col = rec % width
    col_at = lax.broadcasted_iota(jnp.int32, (width, nrec), 0) == col
    for f in range(4):
        rest = res_ref[0, f : f + 1, :] if f < 3 else jnp.ones((1, nrec), f32)
        for piece in range(3 if f < 3 else 1):
            bits = rest.astype(jnp.bfloat16).astype(f32)
            rest = rest - bits
            ct[3 * f + piece] = jnp.where(col_at, bits, 0.0).astype(jnp.bfloat16)

    def receivers(fields):
        def plane(d, carry):
            at = lax.broadcasted_iota(jnp.int32, (depth * tx, nrec), 0) + d * (depth * tx)
            hot = jnp.where(at == row, 1.0, 0.0).astype(jnp.bfloat16)
            for f in fields:
                total = None
                for piece in range(3 if f < 3 else 1):
                    term = lax.dot_general(
                        hot, ct[3 * f + piece], (((1,), (1,)), ((), ())), preferred_element_type=f32
                    )
                    total = term if total is None else total + term
                for i in range(depth):
                    qd[f, d, i] = total[i * tx : i * tx + tx]
            return carry

        lax.fori_loop(0, tiles, plane, 0)

    receivers((2, 1))

    lane = lax.broadcasted_iota(jnp.int32, (tx, width), 1)

    def lap(c, below, above, before, after):
        big = jnp.concatenate([before, c, after], axis=0)
        n = below + above
        n = n + pltpu.roll(big, 1, 0)[8 : tx + 8]
        n = n + pltpu.roll(big, tx + 15, 0)[8 : tx + 8]
        n = n + jnp.where(lane == 0, 0.0, pltpu.roll(c, 1, 1))
        n = n + jnp.where(lane == width - 1, 0.0, pltpu.roll(c, width - 1, 1))
        return n - 6.0 * c

    def cells(field, halos, d, i, j):
        c = field[i, d]
        before = jnp.where(j == 0, 0.0, field[(i + tiles - 1) % tiles, d, tx - 8 : tx])
        after = jnp.where(j == tiles - 1, 0.0, field[(i + 1) % tiles, d, 0:8])
        edge_low = isinstance(d, int) and d == 0
        edge_high = isinstance(d, int) and d == depth - 1
        below = jnp.where(k == 0, 0.0, halos[0, i]) if edge_low else field[i, d - 1]
        above = jnp.where(k == slabs - 1, 0.0, halos[1, i]) if edge_high else field[i, d + 1]
        return c, lap(c, below, above, before, after)

    def interior(body):
        def plane(d, carry):
            def one(j, inner):
                body(d, j)
                return inner

            return lax.fori_loop(0, tiles, one, carry, unroll=2)

        lax.fori_loop(1, depth - 1, plane, 0)

    def p1_cell(d, j):
        c, l = cells(ac, ach, d, j, j)
        p1[j, d] = 2.0 * c - ap[j, d] + co[j, d] * l + qd[2, j, d]

    def p1_sends(j):
        return (
            remote(p1.at[j, depth - 1], p1h.at[0, j], p_s.at[0, j], p_r.at[0, j], (z, up)),
            remote(p1.at[j, 0], p1h.at[1, j], p_s.at[1, j], p_r.at[1, j], (z, down)),
        )

    wait(l_cur)
    wait(l_co)
    wait(l_ap)
    interior(p1_cell)
    for copy in halos_c:
        copy.wait_recv()

    def p1_edge(j, carry):
        p1_cell(0, j)
        p1_cell(depth - 1, j)
        for copy in p1_sends(j):
            copy.start()
        return carry

    lax.fori_loop(0, tiles, p1_edge, 0)

    def ad_cell(d, j):
        c, l = cells(p1, p1h, d, j, j)
        ad[j, d] = 2.0 * c - ac[j, d] + co[j, d] * l + qd[1, j, d]

    interior(ad_cell)

    def ad_edge(j, carry):
        for copy in p1_sends(j):
            copy.wait_recv()
        ad_cell(0, j)
        ad_cell(depth - 1, j)
        return carry

    lax.fori_loop(0, tiles, ad_edge, 0)
    o_ad = [pltpu.make_async_copy(ad.at[j], adj_out.at[0, :, strip(j)], outs.at[0, j]) for j in range(tiles)]
    for copy in o_ad:
        copy.start()

    wait(l_a1)
    wait(l_a0)
    wait(l_a2)

    def place(r):
        return (r - start) & (tiles - 1)

    def send1(r):
        dev = (pair_a if r in FIRST else pair_b, k)
        return remote(img.at[r], v1.at[r], z1_s.at[r], z1_r.at[r], dev)

    def send2(r):
        dev = (pair_b if r in FIRST else pair_a, k)
        return remote(s2.at[r], w2.at[r], z2_s.at[r], z2_r.at[r], dev)

    for r in ORDER:
        at = place(r)

        def image(d, carry, r=r, at=at):
            img[r, d] = ax[1, at, d] * p1[at, d] + ax[0, at, d] * ad[at, d]
            return carry

        lax.fori_loop(0, depth, image, 0, unroll=True)
        send1(r).start()

    receivers((0, 3))
    st_a.wait_recv()
    st_b.wait_recv()

    def group(slot, r):
        cell = jnp.where(stv[slot] > r, 1, 0)
        across = jnp.concatenate([cell] * (width // 128), axis=1)
        return jnp.concatenate([across] * (tx // 8), axis=0)

    for r in ORDER:
        first, second = (1, 2) if r in FIRST else (2, 1)
        send1(r).wait_recv()
        g_own, g_src, g_dst = group(0, r), group(first, r), group(second, r)
        own_dst = g_own == g_dst
        src_dst = g_src == g_dst
        src_own = g_src == g_own

        def combine(d, carry, r=r, own_dst=own_dst, src_dst=src_dst, src_own=src_own):
            mine = img[r, d]
            theirs = v1[r, d]
            s2[r, d] = jnp.where(own_dst, mine, 0.0) + jnp.where(src_dst, theirs, 0.0)
            part[r, d] = mine + jnp.where(src_own, theirs, 0.0)
            return carry

        lax.fori_loop(0, depth, combine, 0, unroll=True)
        send2(r).start()

    half = tiles // 2

    def extra(e):
        if e < half // 2:
            dest = (1 - par) * pair_a + par * pair_b
        else:
            dest = par * pair_a + (1 - par) * pair_b
        return remote(exs.at[e], exr.at[e], ex_s.at[e], ex_r.at[e], (dest, k)), dest

    def source(r, e_low):
        return r, e_low

    for e in range(half):
        copy, dest = extra(e)
        low = e < half // 2
        r_send = (1 - par) * half + e
        r_own = par * half + e
        src_send = jnp.where((par == 1) if low else (par == 0), group(1, r_send), group(2, r_send))
        src_own = jnp.where((par == 0) if low else (par == 1), group(1, r_own), group(2, r_own))
        want_send = dest // 2
        want_own = z // 2
        m_send = group(0, r_send) == want_send
        t_send = src_send == want_send
        m_own = group(0, r_own) == want_own
        t_own = src_own == want_own

        def spread(d, carry, e=e, r_send=r_send, r_own=r_own, m_send=m_send, t_send=t_send, m_own=m_own, t_own=t_own):
            exs[e, d] = jnp.where(m_send, img[r_send, d], 0.0) + jnp.where(t_send, v1[r_send, d], 0.0)
            own[e, d] = jnp.where(m_own, img[r_own, d], 0.0) + jnp.where(t_own, v1[r_own, d], 0.0)
            return carry

        lax.fori_loop(0, depth, spread, 0, unroll=2)
        copy.start()

    def fold(m):
        m = sum(m[:, 128 * i : 128 * i + 128] for i in range(width // 128))
        return sum(m[8 * i : 8 * i + 8] for i in range(tx // 8))

    def tally(carry, t, d, at, b):
        num, den = carry
        return num + fold(qd[t, at, d] * b), den + fold(qd[3, at, d] * b * b)

    def halo_sends(level, field, halos, r):
        return (
            remote(field.at[r, depth - 1], halos.at[0, r], b_s.at[level, 0, r], b_r.at[level, 0, r], (z, up)),
            remote(field.at[r, 0], halos.at[1, r], b_s.at[level, 1, r], b_r.at[level, 1, r], (z, down)),
        )

    zero = jnp.zeros((8, 128), f32)
    sums = (zero, zero)
    for r in ORDER:
        send2(r).wait_recv()
        at = place(r)

        def born1(d, carry, r=r, at=at):
            w = co[at, d] * (part[r, d] + w2[r, d])
            wt[r, d] = w
            b = w * ax[0, at, d]
            b1[r, d] = b
            return tally(carry, 0, d, at, b)

        sums = lax.fori_loop(0, depth, born1, sums, unroll=2)
        for copy in halo_sends(0, b1, b1h, r):
            copy.start()

    def b2_cell(d, r, carry):
        j = place(r)
        c, l = cells(b1, b1h, d, r, j)
        b = 2.0 * c + co[j, d] * l + wt[r, d] * ax[1, j, d]
        b2[r, d] = b
        return tally(carry, 1, d, j, b)

    def b3_cell(d, j, carry):
        r = (j + start) & (tiles - 1)
        c, l = cells(b2, b2h, d, r, j)
        b = 2.0 * c - b1[r, d] + co[j, d] * l + wt[r, d] * ax[2, j, d]
        b3[j, d] = b
        return tally(carry, 2, d, j, b)

    def sweep(cell, carry):
        def plane(d, inner):
            return lax.fori_loop(0, tiles, lambda r, deep: cell(d, r, deep), inner, unroll=2)

        return lax.fori_loop(1, depth - 1, plane, carry)

    sums = sweep(b2_cell, sums)

    def b2_edge(r, carry):
        for copy in halo_sends(0, b1, b1h, r):
            copy.wait_recv()
        carry = b2_cell(0, r, carry)
        carry = b2_cell(depth - 1, r, carry)
        for copy in halo_sends(1, b2, b2h, r):
            copy.start()
        return carry

    sums = lax.fori_loop(0, tiles, b2_edge, sums)
    sums = sweep(b3_cell, sums)

    def b2_wait(r, carry):
        for copy in halo_sends(1, b2, b2h, r):
            copy.wait_recv()
        return carry

    lax.fori_loop(0, tiles, b2_wait, 0)

    def b3_edge(j, carry):
        carry = b3_cell(0, j, carry)
        return b3_cell(depth - 1, j, carry)

    sums = lax.fori_loop(0, tiles, b3_edge, sums)
    o_born = [pltpu.make_async_copy(b3.at[j], born_out.at[0, :, strip(j)], outs.at[1, j]) for j in range(tiles)]
    for copy in o_born:
        copy.start()

    num, den = sums
    for at, (n, coord, partners) in enumerate(phases):
        ar[at, coord, 0] = num
        ar[at, coord, 1] = den
        for d, dev in enumerate(partners):
            remote(ar.at[at, coord], ar.at[at, coord], ar_s.at[at, d], ar_r.at[at, coord], dev).start()
        for d, dev in enumerate(partners):
            other = (coord + 1 + d) % n
            remote(ar.at[at, other], ar.at[at, other], ar_s.at[at, d], ar_r.at[at, other], dev).wait_recv()
        num = ar[at, 0, 0]
        den = ar[at, 0, 1]
        for slot in range(1, n):
            num = num + ar[at, slot, 0]
            den = den + ar[at, slot, 1]
    num = jnp.sum(jnp.sum(num, axis=1, keepdims=True), axis=0, keepdims=True)
    den = jnp.sum(jnp.sum(den, axis=1, keepdims=True), axis=0, keepdims=True)
    alpha = num / (den + 1e-6)

    l_mo.wait()
    for e in range(half):
        extra(e)[0].wait_recv()

        def update(d, carry, e=e):
            cells = slice(e * tx, e * tx + tx)
            nm[d, cells, :] = mo[d, cells, :] - alpha * (own[e, d] + exr[e, d])
            return carry

        lax.fori_loop(0, depth, update, 0, unroll=2)
    o_nm = pltpu.make_async_copy(nm, nm_out, outs.at[2, 0])
    o_nm.start()

    for copy in halos_c:
        copy.wait_send()
    st_a.wait_send()
    st_b.wait_send()

    def drain(j, carry):
        for copy in p1_sends(j):
            copy.wait_send()
        for copy in halo_sends(0, b1, b1h, j):
            copy.wait_send()
        for copy in halo_sends(1, b2, b2h, j):
            copy.wait_send()
        return carry

    lax.fori_loop(0, tiles, drain, 0)
    for r in range(tiles):
        send1(r).wait_send()
        send2(r).wait_send()
    for e in range(half):
        extra(e)[0].wait_send()
    for at, (n, coord, partners) in enumerate(phases):
        for d, dev in enumerate(partners):
            remote(ar.at[at, coord], ar.at[at, coord], ar_s.at[at, d], ar_r.at[at, coord], dev).wait_send()
    wait(o_ad)
    wait(o_born)
    o_nm.wait()


def local(courant, adj_prev, adj_cur, accel, res_data, rec_index, intersection, model):
    shots, slabs = lax.axis_size("shot"), lax.axis_size("slab")
    depth, wide, width = courant.shape[1:]
    tiles = intersection.shape[1]
    tx = wide // tiles
    nrec = rec_index.shape[1]
    f32 = jnp.float32
    dims = (shots, slabs, depth, wide, width, tiles, tx, nrec)
    tiled = (tiles, depth, tx, width)
    part = (tiles // 2, depth, tx, width)
    nph = len(radices(slabs)) + 1
    dma = pltpu.SemaphoreType.DMA
    vm = pltpu.VMEM
    scratch = [
        vm(tiled, f32), vm((2, tiles, tx, width), f32), vm(tiled, f32), vm(tiled, f32), vm((3,) + tiled, f32),
        vm(model.shape, f32), vm(tiled, f32), vm((2, tiles, tx, width), f32), vm(tiled, f32),
        vm(tiled, f32), vm(tiled, f32), vm(tiled, f32), vm(tiled, f32), vm(tiled, f32),
        vm((4,) + tiled, f32), vm((10, width, nrec), jnp.bfloat16),
        vm(tiled, f32), vm((2, tiles, tx, width), f32), vm(tiled, f32), vm((2, tiles, tx, width), f32), vm(tiled, f32),
        vm(tiled, f32), vm(part, f32), vm(part, f32), vm(part, f32), vm(model.shape, f32),
        vm((3, 8, 128), jnp.int32), vm((nph, 4, 2, 8, 128), f32),
        dma((7, tiles)), dma((3, tiles)), dma((2, tiles)), dma((2, tiles)), dma((2, tiles)), dma((2, tiles)),
        dma((2, 2, tiles)), dma((2, 2, tiles)), dma((2,)), dma((2,)),
        dma((tiles,)), dma((tiles,)), dma((tiles,)), dma((tiles,)),
        dma((tiles // 2,)), dma((tiles // 2,)), dma((nph, 4)), dma((nph, 4)),
    ]
    any_spec = pl.BlockSpec(memory_space=pl.ANY)
    vm_spec = pl.BlockSpec(memory_space=pltpu.VMEM)
    return pl.pallas_call(
        functools.partial(kernel, dims),
        out_shape=(
            jax.ShapeDtypeStruct(model.shape, f32),
            jax.ShapeDtypeStruct(courant.shape, f32),
            jax.ShapeDtypeStruct(courant.shape, f32),
        ),
        in_specs=[pl.BlockSpec(memory_space=pltpu.SMEM), vm_spec, vm_spec] + [any_spec] * 5,
        out_specs=(any_spec,) * 3,
        scratch_shapes=scratch,
        compiler_params=pltpu.CompilerParams(
            collective_id=0, has_side_effects=True, vmem_limit_bytes=60 * 1024 * 1024
        ),
    )(intersection, res_data, rec_index, courant, adj_prev, adj_cur, accel, model)


def solution(mesh):
    in_specs = (
        P("shot", "slab", None, None),
        P("shot", "slab", None, None),
        P("shot", "slab", None, None),
        P("shot", None, "slab", None, None),
        P("shot", None, None),
        P("shot", None),
        P("shot", None),
        P("slab", "shot", None),
    )
    out_specs = (
        P("slab", "shot", None),
        P("shot", "slab", None, None),
        P("shot", "slab", None, None),
    )
    return jax.shard_map(local, mesh=mesh, in_specs=in_specs, out_specs=out_specs, check_vma=False)
```

time: 382 us -> 103 us (0.27)
  blocking collectives: 123 us -> 0 us
  Pallas kernels: 0 us -> 95.2 us
  local copies, waits for them, and re-layouts: 95.3 us -> 7.38 us
  other arithmetic: 59 us -> 0 us
  waiting for transfers between devices: 51.8 us -> 0 us
  starting transfers between devices: 21.8 us -> 0 us
  between operations: 19.4 us -> 0.65 us
  matrix products: 8.8 us -> 0 us
    pallas_call x0 -> x1, Pallas kernels: none -> 95.2 us  [local(): pl.pallas_call(functools.partial(kernel, dims), out_shape=(jax.ShapeDtype...]
    psum x1 -> x0, blocking collectives: 67.4 us -> none  [local(): num_all, den_all = lax.psum((num, den), ('shot', 'slab'))]
    gather x3 -> x0, local copies, waits for them, and re-layouts: 61.6 us -> none  [sample(): return jnp.where(inside, field.reshape(-1)[where], 0.0)]
    all_to_all x1 -> x0, blocking collectives: 55.2 us -> none  [local(): lax.all_to_all(outbox, 'shot', split_axis=1, concat_axis=1, tiled=True)]
    all_gather x1 -> x0, waiting for transfers between devices: 49.9 us -> none  [local(): whole = lax.all_gather(owned, 'shot', axis=1, tiled=True)]
    add x5 -> x0, other arithmetic: 34.8 us -> none  [the longest x2 17.5 us: wave_step(): return 2.0 * ext[1:-1] - before + coeff * lap_inner(ext)]
    ppermute x8 -> x0, starting transfers between devices: 21.8 us -> none  [the longest x4 16.3 us: extended(): before = lax.ppermute(last, axis, up)]
    scatter-add x2 -> x0, other arithmetic: 11.7 us -> none  [inject(): field.reshape(-1).at[where].add(jnp.where(inside, values, 0.0))]
  transfers between devices with their start and end apart: 9 -> 0, of which waited for: 3 -> 0; matrix products, arithmetic and copies ran while one was open for 16% -> 0% of each run, Pallas kernels for 0% -> 0%
where the time goes in v1:
time: 103 us
  Pallas kernels  95.2 us (92%)
  local copies, waits for them, and re-layouts  7.38 us (7%)
    pallas_call x1, Pallas kernels, local(): pl.pallas_call(functools.partial(kernel, dims), out_shape=(jax.ShapeDtype...  95.2 us
    unnamed x8, local copies, waits for them, and re-layouts  7.38 us

profile of v1, /device:TPU:0, one launch (start us, length us, event | category | flops | bytes accessed | tf_op | source)
XLA Modules:
  0.0 103.2 jit_solution(5228041975352862288)
XLA Ops:
  0.6 1.3 %copy.11.res_ref = f32[1,3,512]{2,1,0:T(4,128)} copy(f32[1,3,512]{2,0,1:T(1,128)} %param.12) | data formatting | bytes 12288 | tf_op args[4]
  1.9 95.2 %shard_map.103 = (f32[8,128,256]{2,1,0:T(8,128)}, f32[1,8,256,256]{3,2,1,0:T(8,128)}, f32[1,8,256,256]{3,2,1,0:T(8,128)}) custom-call(s32[1,8]{1,0:T(1,128)} %inter_ref.1, f32[1,3,512]{2,1,0:T(4,128)} %copy.11.res_ref, s32[1,512]{1,0:T(1,128)} %rec_ref.1, f32[1,8,256,256]{3,2,1,0:T(8,128)} %courant.1, f32[1,8,256,256]{3,2,1,0:T(8,128)} %prev.1, ...), custom_call_target="tpu_custom_call" | custom-call | tf_op jit(solution)/shard_map/pallas_call | solution.py:461
  97.1 0.0 copy-start.1
  97.1 2.4 %copy.15 = f32[8,128,256]{2,1,0:T(8,128)} copy(f32[8,128,256]{2,1,0:T(8,128)} %get-tuple-element.6) | data formatting | bytes 2097152
  99.5 0.0 copy-done.1
  99.5 0.0 copy-start
  99.6 1.3 %copy.16 = f32[1,8,256,256]{3,2,1,0:T(8,128)} copy(f32[1,8,256,256]{3,2,1,0:T(8,128)S(1)} %copy-done.1) | data formatting | bytes 4194304
  100.9 1.0 copy-done
  101.9 1.3 %copy.17 = f32[1,8,256,256]{3,2,1,0:T(8,128)} copy(f32[1,8,256,256]{3,2,1,0:T(8,128)S(1)} %copy-done) | data formatting | bytes 4194304
Async XLA Ops:
  97.1 2.4 %copy-start.1 = (f32[1,8,256,256]{3,2,1,0:T(8,128)S(1)}, f32[1,8,256,256]{3,2,1,0:T(8,128)}, u32[]{:S(2)}) copy-start(f32[1,8,256,256]{3,2,1,0:T(8,128)} %get-tuple-element.7) | copy-start | bytes 6291460
  99.5 2.3 %copy-start = (f32[1,8,256,256]{3,2,1,0:T(8,128)S(1)}, f32[1,8,256,256]{3,2,1,0:T(8,128)}, u32[]{:S(2)}) copy-start(f32[1,8,256,256]{3,2,1,0:T(8,128)} %get-tuple-element.8) | copy-start | bytes 6291460

commit v2 on v1

--- a/solution.py
+++ b/solution.py
@@ -12,22 +12,13 @@
 FIRST = (0, 1, 6, 7)
 
 
-def radices(count):
-    out = []
-    while count > 1:
-        step = 4 if count % 4 == 0 and (out or count == 4) else 2
-        out.append(step)
-        count //= step
-    return out
-
-
 def kernel(
     dims,
     inter_ref, res_ref, rec_ref, courant, prev, cur, accel, model,
-    nm_out, adj_out, born_out,
+    nm, adj, born,
     ac, ach, co, ap, ax, mo, p1, p1h, ad, img, v1, s2, w2, part,
-    qd, ct, b1, b1h, b2, b2h, b3, wt, exs, exr, own, nm, stv, ar,
-    ld, outs, h_s, h_r, p_s, p_r, b_s, b_r, st_s, st_r, z1_s, z1_r, z2_s, z2_r, ex_s, ex_r, ar_s, ar_r,
+    qd, ct, b1, b1h, b2, b2h, wt, exs, exr, own, stv, ar,
+    ld, h_s, h_r, p_s, p_r, b_s, b_r, st_s, st_r, z1_s, z1_r, z2_s, z2_r, ex_s, ex_r, ar_s, ar_r,
 ):
     shots, slabs, depth, wide, width, tiles, tx, nrec = dims
     f32 = jnp.float32
@@ -39,14 +30,21 @@
     up = (k + 1) % slabs
     down = (k + slabs - 1) % slabs
 
-    phases = []
-    stride = 1
-    for n in radices(slabs):
-        coord = (k // stride) % n
-        base = k - coord * stride
-        phases.append((n, coord, [(z, base + ((coord + d) % n) * stride) for d in range(1, n)]))
-        stride *= n
-    phases.append((shots, z, [((z + d) % shots, k) for d in range(1, shots)]))
+    core = k % 2
+    chip = k // 2
+    chips = slabs // 2
+    phases = (
+        (chips, chip, [(z, (chip + d) % chips * 2 + core) for d in range(1, chips)]),
+        (
+            2 * shots,
+            2 * z + core,
+            [((2 * z + core + d) % (2 * shots) // 2, chip * 2 + (core + d) % 2) for d in range(1, 2 * shots)],
+        ),
+    )
+    middle = list(range(2, depth - 2))
+    outer = [0, 1, depth - 2, depth - 1]
+    parts = (slice(0, depth - 4), slice(depth - 4, depth))
+    slots = (list(enumerate(middle)), [(depth - 4 + i, d) for i, d in enumerate(outer)])
 
     barrier = pltpu.get_barrier_semaphore()
     greet = [(z, up), (z, down)] + [dev for phase in phases for dev in phase[2]]
@@ -104,7 +102,7 @@
     col = rec % width
     col_at = lax.broadcasted_iota(jnp.int32, (width, nrec), 0) == col
     for f in range(4):
-        rest = res_ref[0, f : f + 1, :] if f < 3 else jnp.ones((1, nrec), f32)
+        rest = jnp.concatenate([res_ref[f, i : i + 1, :] for i in range(nrec // 128)], axis=1) if f < 3 else jnp.ones((1, nrec), f32)
         for piece in range(3 if f < 3 else 1):
             bits = rest.astype(jnp.bfloat16).astype(f32)
             rest = rest - bits
@@ -150,7 +148,7 @@
         above = jnp.where(k == slabs - 1, 0.0, halos[1, i]) if edge_high else field[i, d + 1]
         return c, lap(c, below, above, before, after)
 
-    def interior(body):
+    def planes(body, first, last):
         def plane(d, carry):
             def one(j, inner):
                 body(d, j)
@@ -158,7 +156,7 @@
 
             return lax.fori_loop(0, tiles, one, carry, unroll=2)
 
-        lax.fori_loop(1, depth - 1, plane, 0)
+        lax.fori_loop(first, last, plane, 0)
 
     def p1_cell(d, j):
         c, l = cells(ac, ach, d, j, j)
@@ -170,10 +168,39 @@
             remote(p1.at[j, 0], p1h.at[1, j], p_s.at[1, j], p_r.at[1, j], (z, down)),
         )
 
+    def ad_cell(d, j):
+        c, l = cells(p1, p1h, d, j, j)
+        a = 2.0 * c - ac[j, d] + co[j, d] * l + qd[1, j, d]
+        ad[j, d] = a
+        adj[0, d, pl.ds(pl.multiple_of(j * tx, tx), tx), :] = a
+
+    def place(r):
+        return (r - start) & (tiles - 1)
+
+    def send1(r, h):
+        dev = (pair_a if r in FIRST else pair_b, k)
+        return remote(img.at[r, parts[h]], v1.at[r, parts[h]], z1_s.at[r, h], z1_r.at[r, h], dev)
+
+    def send2(r, h):
+        dev = (pair_b if r in FIRST else pair_a, k)
+        return remote(s2.at[r, parts[h]], w2.at[r, parts[h]], z2_s.at[r, h], z2_r.at[r, h], dev)
+
+    def images(h):
+        for r in ORDER:
+            at = place(r)
+            for slot, d in slots[h]:
+                img[r, slot] = ax[1, at, d] * p1[at, d] + ax[0, at, d] * ad[at, d]
+            send1(r, h).start()
+
     wait(l_cur)
     wait(l_co)
     wait(l_ap)
-    interior(p1_cell)
+    planes(p1_cell, 1, depth - 1)
+    planes(ad_cell, 2, depth - 2)
+    wait(l_a1)
+    wait(l_a0)
+    wait(l_a2)
+    images(0)
     for copy in halos_c:
         copy.wait_recv()
 
@@ -185,12 +212,8 @@
         return carry
 
     lax.fori_loop(0, tiles, p1_edge, 0)
-
-    def ad_cell(d, j):
-        c, l = cells(p1, p1h, d, j, j)
-        ad[j, d] = 2.0 * c - ac[j, d] + co[j, d] * l + qd[1, j, d]
-
-    interior(ad_cell)
+    planes(ad_cell, 1, 2)
+    planes(ad_cell, depth - 2, depth - 1)
 
     def ad_edge(j, carry):
         for copy in p1_sends(j):
@@ -200,34 +223,7 @@
         return carry
 
     lax.fori_loop(0, tiles, ad_edge, 0)
-    o_ad = [pltpu.make_async_copy(ad.at[j], adj_out.at[0, :, strip(j)], outs.at[0, j]) for j in range(tiles)]
-    for copy in o_ad:
-        copy.start()
-
-    wait(l_a1)
-    wait(l_a0)
-    wait(l_a2)
-
-    def place(r):
-        return (r - start) & (tiles - 1)
-
-    def send1(r):
-        dev = (pair_a if r in FIRST else pair_b, k)
-        return remote(img.at[r], v1.at[r], z1_s.at[r], z1_r.at[r], dev)
-
-    def send2(r):
-        dev = (pair_b if r in FIRST else pair_a, k)
-        return remote(s2.at[r], w2.at[r], z2_s.at[r], z2_r.at[r], dev)
-
-    for r in ORDER:
-        at = place(r)
-
-        def image(d, carry, r=r, at=at):
-            img[r, d] = ax[1, at, d] * p1[at, d] + ax[0, at, d] * ad[at, d]
-            return carry
-
-        lax.fori_loop(0, depth, image, 0, unroll=True)
-        send1(r).start()
+    images(1)
 
     receivers((0, 3))
     st_a.wait_recv()
@@ -238,23 +234,23 @@
         across = jnp.concatenate([cell] * (width // 128), axis=1)
         return jnp.concatenate([across] * (tx // 8), axis=0)
 
+    for h in range(2):
+        for r in ORDER:
+            first, second = (1, 2) if r in FIRST else (2, 1)
+            send1(r, h).wait_recv()
+            g_own, g_src, g_dst = group(0, r), group(first, r), group(second, r)
+            own_dst = g_own == g_dst
+            src_dst = g_src == g_dst
+            src_own = g_src == g_own
+            for slot, _ in slots[h]:
+                mine = img[r, slot]
+                theirs = v1[r, slot]
+                s2[r, slot] = jnp.where(own_dst, mine, 0.0) + jnp.where(src_dst, theirs, 0.0)
+                part[r, slot] = mine + jnp.where(src_own, theirs, 0.0)
+            if h == 1:
+                send2(r, 1).start()
     for r in ORDER:
-        first, second = (1, 2) if r in FIRST else (2, 1)
-        send1(r).wait_recv()
-        g_own, g_src, g_dst = group(0, r), group(first, r), group(second, r)
-        own_dst = g_own == g_dst
-        src_dst = g_src == g_dst
-        src_own = g_src == g_own
-
-        def combine(d, carry, r=r, own_dst=own_dst, src_dst=src_dst, src_own=src_own):
-            mine = img[r, d]
-            theirs = v1[r, d]
-            s2[r, d] = jnp.where(own_dst, mine, 0.0) + jnp.where(src_dst, theirs, 0.0)
-            part[r, d] = mine + jnp.where(src_own, theirs, 0.0)
-            return carry
-
-        lax.fori_loop(0, depth, combine, 0, unroll=True)
-        send2(r).start()
+        send2(r, 0).start()
 
     half = tiles // 2
 
@@ -264,9 +260,6 @@
         else:
             dest = par * pair_a + (1 - par) * pair_b
         return remote(exs.at[e], exr.at[e], ex_s.at[e], ex_r.at[e], (dest, k)), dest
-
-    def source(r, e_low):
-        return r, e_low
 
     for e in range(half):
         copy, dest = extra(e)
@@ -306,20 +299,23 @@
 
     zero = jnp.zeros((8, 128), f32)
     sums = (zero, zero)
-    for r in ORDER:
-        send2(r).wait_recv()
-        at = place(r)
-
-        def born1(d, carry, r=r, at=at):
-            w = co[at, d] * (part[r, d] + w2[r, d])
-            wt[r, d] = w
-            b = w * ax[0, at, d]
-            b1[r, d] = b
-            return tally(carry, 0, d, at, b)
-
-        sums = lax.fori_loop(0, depth, born1, sums, unroll=2)
-        for copy in halo_sends(0, b1, b1h, r):
-            copy.start()
+
+    def born1(h, carry):
+        for r in ORDER:
+            send2(r, h).wait_recv()
+            at = place(r)
+            for slot, d in slots[h]:
+                w = co[at, d] * (part[r, slot] + w2[r, slot])
+                wt[r, d] = w
+                b = w * ax[0, at, d]
+                b1[r, d] = b
+                carry = tally(carry, 0, d, at, b)
+            if h == 1:
+                for copy in halo_sends(0, b1, b1h, r):
+                    copy.start()
+        return carry
+
+    sums = born1(1, sums)
 
     def b2_cell(d, r, carry):
         j = place(r)
@@ -332,7 +328,7 @@
         r = (j + start) & (tiles - 1)
         c, l = cells(b2, b2h, d, r, j)
         b = 2.0 * c - b1[r, d] + co[j, d] * l + wt[r, d] * ax[2, j, d]
-        b3[j, d] = b
+        born[0, d, pl.ds(pl.multiple_of(j * tx, tx), tx), :] = b
         return tally(carry, 2, d, j, b)
 
     def sweep(cell, carry):
@@ -340,8 +336,6 @@
             return lax.fori_loop(0, tiles, lambda r, deep: cell(d, r, deep), inner, unroll=2)
 
         return lax.fori_loop(1, depth - 1, plane, carry)
-
-    sums = sweep(b2_cell, sums)
 
     def b2_edge(r, carry):
         for copy in halo_sends(0, b1, b1h, r):
@@ -353,6 +347,8 @@
         return carry
 
     sums = lax.fori_loop(0, tiles, b2_edge, sums)
+    sums = born1(0, sums)
+    sums = sweep(b2_cell, sums)
     sums = sweep(b3_cell, sums)
 
     def b2_wait(r, carry):
@@ -367,40 +363,32 @@
         return b3_cell(depth - 1, j, carry)
 
     sums = lax.fori_loop(0, tiles, b3_edge, sums)
-    o_born = [pltpu.make_async_copy(b3.at[j], born_out.at[0, :, strip(j)], outs.at[1, j]) for j in range(tiles)]
-    for copy in o_born:
-        copy.start()
-
-    num, den = sums
+
+    row_at = lax.broadcasted_iota(jnp.int32, (8, 128), 0)
+    num = jnp.sum(sums[0], axis=0, keepdims=True)
+    den = jnp.sum(sums[1], axis=0, keepdims=True)
+    total = jnp.where(row_at == 0, num, jnp.where(row_at == 1, den, 0.0))
     for at, (n, coord, partners) in enumerate(phases):
-        ar[at, coord, 0] = num
-        ar[at, coord, 1] = den
+        ar[at, coord] = total
         for d, dev in enumerate(partners):
             remote(ar.at[at, coord], ar.at[at, coord], ar_s.at[at, d], ar_r.at[at, coord], dev).start()
         for d, dev in enumerate(partners):
             other = (coord + 1 + d) % n
             remote(ar.at[at, other], ar.at[at, other], ar_s.at[at, d], ar_r.at[at, other], dev).wait_recv()
-        num = ar[at, 0, 0]
-        den = ar[at, 0, 1]
+        total = ar[at, 0]
         for slot in range(1, n):
-            num = num + ar[at, slot, 0]
-            den = den + ar[at, slot, 1]
-    num = jnp.sum(jnp.sum(num, axis=1, keepdims=True), axis=0, keepdims=True)
-    den = jnp.sum(jnp.sum(den, axis=1, keepdims=True), axis=0, keepdims=True)
+            total = total + ar[at, slot]
+    num = jnp.sum(total[0:1], axis=1, keepdims=True)
+    den = jnp.sum(total[1:2], axis=1, keepdims=True)
     alpha = num / (den + 1e-6)
 
     l_mo.wait()
     for e in range(half):
         extra(e)[0].wait_recv()
 
-        def update(d, carry, e=e):
-            cells = slice(e * tx, e * tx + tx)
-            nm[d, cells, :] = mo[d, cells, :] - alpha * (own[e, d] + exr[e, d])
-            return carry
-
-        lax.fori_loop(0, depth, update, 0, unroll=2)
-    o_nm = pltpu.make_async_copy(nm, nm_out, outs.at[2, 0])
-    o_nm.start()
+        for slot, d in slots[0] + slots[1]:
+            cells_at = slice(e * tx, e * tx + tx)
+            nm[d, cells_at, :] = mo[d, cells_at, :] - alpha * (own[e, slot] + exr[e, slot])
 
     for copy in halos_c:
         copy.wait_send()
@@ -418,17 +406,14 @@
 
     lax.fori_loop(0, tiles, drain, 0)
     for r in range(tiles):
-        send1(r).wait_send()
-        send2(r).wait_send()
+        for h in range(2):
+            send1(r, h).wait_send()
+            send2(r, h).wait_send()
     for e in range(half):
         extra(e)[0].wait_send()
     for at, (n, coord, partners) in enumerate(phases):
         for d, dev in enumerate(partners):
             remote(ar.at[at, coord], ar.at[at, coord], ar_s.at[at, d], ar_r.at[at, coord], dev).wait_send()
-    wait(o_ad)
-    wait(o_born)
-    o_nm.wait()
-
 
 def local(courant, adj_prev, adj_cur, accel, res_data, rec_index, intersection, model):
     shots, slabs = lax.axis_size("shot"), lax.axis_size("slab")
@@ -440,38 +425,39 @@
     dims = (shots, slabs, depth, wide, width, tiles, tx, nrec)
     tiled = (tiles, depth, tx, width)
     part = (tiles // 2, depth, tx, width)
-    nph = len(radices(slabs)) + 1
+    most = max(slabs // 2, 2 * shots)
     dma = pltpu.SemaphoreType.DMA
     vm = pltpu.VMEM
+    halo = (2, tiles, tx, width)
     scratch = [
-        vm(tiled, f32), vm((2, tiles, tx, width), f32), vm(tiled, f32), vm(tiled, f32), vm((3,) + tiled, f32),
-        vm(model.shape, f32), vm(tiled, f32), vm((2, tiles, tx, width), f32), vm(tiled, f32),
+        vm(tiled, f32), vm(halo, f32), vm(tiled, f32), vm(tiled, f32), vm((3,) + tiled, f32),
+        vm(model.shape, f32), vm(tiled, f32), vm(halo, f32), vm(tiled, f32),
         vm(tiled, f32), vm(tiled, f32), vm(tiled, f32), vm(tiled, f32), vm(tiled, f32),
         vm((4,) + tiled, f32), vm((10, width, nrec), jnp.bfloat16),
-        vm(tiled, f32), vm((2, tiles, tx, width), f32), vm(tiled, f32), vm((2, tiles, tx, width), f32), vm(tiled, f32),
-        vm(tiled, f32), vm(part, f32), vm(part, f32), vm(part, f32), vm(model.shape, f32),
-        vm((3, 8, 128), jnp.int32), vm((nph, 4, 2, 8, 128), f32),
-        dma((7, tiles)), dma((3, tiles)), dma((2, tiles)), dma((2, tiles)), dma((2, tiles)), dma((2, tiles)),
+        vm(tiled, f32), vm(halo, f32), vm(tiled, f32), vm(halo, f32),
+        vm(tiled, f32), vm(part, f32), vm(part, f32), vm(part, f32),
+        vm((3, 8, 128), jnp.int32), vm((2, most, 8, 128), f32),
+        dma((7, tiles)), dma((2, tiles)), dma((2, tiles)), dma((2, tiles)), dma((2, tiles)),
         dma((2, 2, tiles)), dma((2, 2, tiles)), dma((2,)), dma((2,)),
-        dma((tiles,)), dma((tiles,)), dma((tiles,)), dma((tiles,)),
-        dma((tiles // 2,)), dma((tiles // 2,)), dma((nph, 4)), dma((nph, 4)),
+        dma((tiles, 2)), dma((tiles, 2)), dma((tiles, 2)), dma((tiles, 2)),
+        dma((tiles // 2,)), dma((tiles // 2,)), dma((2, most)), dma((2, most)),
     ]
     any_spec = pl.BlockSpec(memory_space=pl.ANY)
     vm_spec = pl.BlockSpec(memory_space=pltpu.VMEM)
     return pl.pallas_call(
         functools.partial(kernel, dims),
         out_shape=(
-            jax.ShapeDtypeStruct(model.shape, f32),
-            jax.ShapeDtypeStruct(courant.shape, f32),
-            jax.ShapeDtypeStruct(courant.shape, f32),
+            pltpu.VMEM(model.shape, f32),
+            pltpu.VMEM(courant.shape, f32),
+            pltpu.VMEM(courant.shape, f32),
         ),
         in_specs=[pl.BlockSpec(memory_space=pltpu.SMEM), vm_spec, vm_spec] + [any_spec] * 5,
-        out_specs=(any_spec,) * 3,
+        out_specs=(vm_spec,) * 3,
         scratch_shapes=scratch,
         compiler_params=pltpu.CompilerParams(
-            collective_id=0, has_side_effects=True, vmem_limit_bytes=60 * 1024 * 1024
+            collective_id=0, has_side_effects=True, vmem_limit_bytes=56 * 1024 * 1024
         ),
-    )(intersection, res_data, rec_index, courant, adj_prev, adj_cur, accel, model)
+    )(intersection, res_data.reshape(3, nrec // 128, 128), rec_index, courant, adj_prev, adj_cur, accel, model)
 
 
 def solution(mesh):

time: 103 us -> 89.5 us (0.87); the launches traced: 103 us -> 88.4 us
  Pallas kernels: 95.2 us -> 84.1 us
  local copies, waits for them, and re-layouts: 7.38 us -> 3.61 us
    pallas_call x1, Pallas kernels: 95.2 us -> 84.1 us  [local(): pl.pallas_call(functools.partial(kernel, dims), out_shape=(pltpu.VMEM(mod...]
    unnamed x8 -> x3, local copies, waits for them, and re-layouts: 7.38 us -> 3.61 us
where the time goes in v2:
time: 89.5 us; the launch traced here: 88.4 us
  Pallas kernels  84.1 us (94%)
  local copies, waits for them, and re-layouts  3.61 us (4%)
    pallas_call x1, Pallas kernels, local(): pl.pallas_call(functools.partial(kernel, dims), out_shape=(pltpu.VMEM(mod...  84.1 us
    unnamed x3, local copies, waits for them, and re-layouts  3.61 us

profile of v2, /device:TPU:0, one launch (start us, length us, event | category | flops | bytes accessed | tf_op | source)
XLA Modules:
  0.0 88.4 jit_solution(16318148295682179856)
XLA Ops:
  0.6 84.1 %shard_map.103 = (f32[8,128,256]{2,1,0:T(8,128)S(1)}, f32[1,8,256,256]{3,2,1,0:T(8,128)S(1)}, f32[1,8,256,256]{3,2,1,0:T(8,128)S(1)}) custom-call(s32[1,8]{1,0:T(1,128)} %inter_ref.1, f32[3,4,128]{2,1,0:T(4,128)} %bitcast.1, s32[1,512]{1,0:T(1,128)} %rec_ref.1, f32[1,8,256,256]{3,2,1,0:T(8,128)} %courant.1, f32[1,8,256,256]{3,2,1,0:T(8,128)} %prev.1, ...), custom_call_target="tpu_custom_call" | custom-call | tf_op jit(solution)/shard_map/pallas_call | solution.py:447
  84.8 1.0 %copy.14 = f32[8,128,256]{2,1,0:T(8,128)} copy(f32[8,128,256]{2,1,0:T(8,128)S(1)} %get-tuple-element.3) | data formatting | bytes 2097152
  85.7 1.3 %copy.15 = f32[1,8,256,256]{3,2,1,0:T(8,128)} copy(f32[1,8,256,256]{3,2,1,0:T(8,128)S(1)} %get-tuple-element.4) | data formatting | bytes 4194304
  87.0 1.3 %copy.16 = f32[1,8,256,256]{3,2,1,0:T(8,128)} copy(f32[1,8,256,256]{3,2,1,0:T(8,128)S(1)} %get-tuple-element.5) | data formatting | bytes 4194304

commit v3 on v2

--- a/solution.py
+++ b/solution.py
@@ -10,6 +10,7 @@
 MESH = pl.DeviceIdType.MESH
 ORDER = (1, 2, 0, 3, 7, 4, 6, 5)
 FIRST = (0, 1, 6, 7)
+READY = {3: (1, 2), 4: (0, 3), 5: (7, 4, 6, 5)}
 
 
 def kernel(
@@ -17,7 +18,7 @@
     inter_ref, res_ref, rec_ref, courant, prev, cur, accel, model,
     nm, adj, born,
     ac, ach, co, ap, ax, mo, p1, p1h, ad, img, v1, s2, w2, part,
-    qd, ct, b1, b1h, b2, b2h, wt, exs, exr, own, stv, ar,
+    qd, ct, hot, b1, b1h, b2, b2h, wt, exs, exr, own, stv, ar,
     ld, h_s, h_r, p_s, p_r, b_s, b_r, st_s, st_r, z1_s, z1_r, z2_s, z2_r, ex_s, ex_r, ar_s, ar_r,
 ):
     shots, slabs, depth, wide, width, tiles, tx, nrec = dims
@@ -81,19 +82,6 @@
     start = inter_ref[0, 0]
     stv[0] = jnp.full(stv.shape[1:], start, jnp.int32)
 
-    pl.semaphore_wait(barrier, len(greet))
-
-    halos_c = []
-    for j in range(tiles):
-        halos_c.append(remote(cur.at[0, depth - 1, strip(j)], ach.at[0, j], h_s.at[0, j], h_r.at[0, j], (z, up)))
-        halos_c.append(remote(cur.at[0, 0, strip(j)], ach.at[1, j], h_s.at[1, j], h_r.at[1, j], (z, down)))
-    for copy in halos_c:
-        copy.start()
-    st_a = remote(stv.at[0], stv.at[1], st_s.at[0], st_r.at[0], (pair_a, k))
-    st_b = remote(stv.at[0], stv.at[2], st_s.at[1], st_r.at[1], (pair_b, k))
-    st_a.start()
-    st_b.start()
-
     rec = rec_ref[...] - k * (depth * wide * width)
     inside = (rec >= 0) & (rec < depth * wide * width)
     line = rec // width
@@ -106,26 +94,49 @@
         for piece in range(3 if f < 3 else 1):
             bits = rest.astype(jnp.bfloat16).astype(f32)
             rest = rest - bits
-            ct[3 * f + piece] = jnp.where(col_at, bits, 0.0).astype(jnp.bfloat16)
+            ct[f, :, piece * nrec : piece * nrec + nrec] = jnp.where(col_at, bits, 0.0).astype(jnp.bfloat16)
+
+    def mark(t, carry):
+        at = lax.broadcasted_iota(jnp.int32, (depth * tx, nrec), 0) + t * (depth * tx)
+        hot[t] = jnp.where(at == row, 1.0, 0.0).astype(jnp.bfloat16)
+        return carry
+
+    lax.fori_loop(0, tiles, mark, 0, unroll=2)
 
     def receivers(fields):
-        def plane(d, carry):
-            at = lax.broadcasted_iota(jnp.int32, (depth * tx, nrec), 0) + d * (depth * tx)
-            hot = jnp.where(at == row, 1.0, 0.0).astype(jnp.bfloat16)
+        def group_of(t, carry):
+            lines = jnp.concatenate([hot[4 * t + i] for i in range(4)], axis=0)
+            triple = jnp.concatenate([lines] * 3, axis=1)
             for f in fields:
-                total = None
-                for piece in range(3 if f < 3 else 1):
-                    term = lax.dot_general(
-                        hot, ct[3 * f + piece], (((1,), (1,)), ((), ())), preferred_element_type=f32
-                    )
-                    total = term if total is None else total + term
-                for i in range(depth):
-                    qd[f, d, i] = total[i * tx : i * tx + tx]
+                total = lax.dot_general(
+                    triple if f < 3 else lines,
+                    ct[f] if f < 3 else ct[f, :, 0:nrec],
+                    (((1,), (1,)), ((), ())),
+                    preferred_element_type=f32,
+                )
+                for i in range(4):
+                    for d in range(depth):
+                        first = (i * depth + d) * tx
+                        qd[f, 4 * t + i, d] = total[first : first + tx]
             return carry
 
-        lax.fori_loop(0, tiles, plane, 0)
+        lax.fori_loop(0, tiles // 4, group_of, 0)
 
     receivers((2, 1))
+
+    pl.semaphore_wait(barrier, len(greet))
+
+    halos_c = []
+    for j in range(tiles):
+        halos_c.append(remote(cur.at[0, depth - 1, strip(j)], ach.at[0, j], h_s.at[0, j], h_r.at[0, j], (z, up)))
+        halos_c.append(remote(cur.at[0, 0, strip(j)], ach.at[1, j], h_s.at[1, j], h_r.at[1, j], (z, down)))
+    for copy in halos_c:
+        copy.start()
+    st_a = remote(stv.at[0], stv.at[1], st_s.at[0], st_r.at[0], (pair_a, k))
+    st_b = remote(stv.at[0], stv.at[2], st_s.at[1], st_r.at[1], (pair_b, k))
+    st_a.start()
+    st_b.start()
+
 
     lane = lax.broadcasted_iota(jnp.int32, (tx, width), 1)
 
@@ -154,7 +165,7 @@
                 body(d, j)
                 return inner
 
-            return lax.fori_loop(0, tiles, one, carry, unroll=2)
+            return lax.fori_loop(0, tiles, one, carry, unroll=4)
 
         lax.fori_loop(first, last, plane, 0)
 
@@ -313,9 +324,10 @@
             if h == 1:
                 for copy in halo_sends(0, b1, b1h, r):
                     copy.start()
-        return carry
-
-    sums = born1(1, sums)
+            elif r in READY:
+                carry = b2_tiles(READY[r], carry)
+        return carry
+
 
     def b2_cell(d, r, carry):
         j = place(r)
@@ -331,9 +343,17 @@
         born[0, d, pl.ds(pl.multiple_of(j * tx, tx), tx), :] = b
         return tally(carry, 2, d, j, b)
 
-    def sweep(cell, carry):
+    def sweep(carry):
         def plane(d, inner):
-            return lax.fori_loop(0, tiles, lambda r, deep: cell(d, r, deep), inner, unroll=2)
+            return lax.fori_loop(0, tiles, lambda j, deep: b3_cell(d, j, deep), inner, unroll=4)
+
+        return lax.fori_loop(1, depth - 1, plane, carry)
+
+    def b2_tiles(chosen, carry):
+        def plane(d, inner):
+            for r in chosen:
+                inner = b2_cell(d, r, inner)
+            return inner
 
         return lax.fori_loop(1, depth - 1, plane, carry)
 
@@ -346,10 +366,30 @@
             copy.start()
         return carry
 
+    sums = born1(1, sums)
     sums = lax.fori_loop(0, tiles, b2_edge, sums)
+    for copy in halos_c:
+        copy.wait_send()
+    st_a.wait_send()
+    st_b.wait_send()
+
+    def drain(j, carry):
+        for copy in p1_sends(j):
+            copy.wait_send()
+        for copy in halo_sends(0, b1, b1h, j):
+            copy.wait_send()
+        for copy in halo_sends(1, b2, b2h, j):
+            copy.wait_send()
+        return carry
+
+    lax.fori_loop(0, tiles, drain, 0)
+    for r in range(tiles):
+        send1(r, 0).wait_send()
+        send1(r, 1).wait_send()
+        send2(r, 1).wait_send()
+
     sums = born1(0, sums)
-    sums = sweep(b2_cell, sums)
-    sums = sweep(b3_cell, sums)
+    sums = sweep(sums)
 
     def b2_wait(r, carry):
         for copy in halo_sends(1, b2, b2h, r):
@@ -372,6 +412,10 @@
         ar[at, coord] = total
         for d, dev in enumerate(partners):
             remote(ar.at[at, coord], ar.at[at, coord], ar_s.at[at, d], ar_r.at[at, coord], dev).start()
+        if at == 0:
+            for r in range(tiles):
+                send2(r, 0).wait_send()
+            l_mo.wait()
         for d, dev in enumerate(partners):
             other = (coord + 1 + d) % n
             remote(ar.at[at, other], ar.at[at, other], ar_s.at[at, d], ar_r.at[at, other], dev).wait_recv()
@@ -382,38 +426,17 @@
     den = jnp.sum(total[1:2], axis=1, keepdims=True)
     alpha = num / (den + 1e-6)
 
-    l_mo.wait()
     for e in range(half):
-        extra(e)[0].wait_recv()
-
+        copy = extra(e)[0]
+        copy.wait_recv()
         for slot, d in slots[0] + slots[1]:
             cells_at = slice(e * tx, e * tx + tx)
             nm[d, cells_at, :] = mo[d, cells_at, :] - alpha * (own[e, slot] + exr[e, slot])
-
-    for copy in halos_c:
         copy.wait_send()
-    st_a.wait_send()
-    st_b.wait_send()
-
-    def drain(j, carry):
-        for copy in p1_sends(j):
-            copy.wait_send()
-        for copy in halo_sends(0, b1, b1h, j):
-            copy.wait_send()
-        for copy in halo_sends(1, b2, b2h, j):
-            copy.wait_send()
-        return carry
-
-    lax.fori_loop(0, tiles, drain, 0)
-    for r in range(tiles):
-        for h in range(2):
-            send1(r, h).wait_send()
-            send2(r, h).wait_send()
-    for e in range(half):
-        extra(e)[0].wait_send()
     for at, (n, coord, partners) in enumerate(phases):
         for d, dev in enumerate(partners):
             remote(ar.at[at, coord], ar.at[at, coord], ar_s.at[at, d], ar_r.at[at, coord], dev).wait_send()
+
 
 def local(courant, adj_prev, adj_cur, accel, res_data, rec_index, intersection, model):
     shots, slabs = lax.axis_size("shot"), lax.axis_size("slab")
@@ -433,7 +456,7 @@
         vm(tiled, f32), vm(halo, f32), vm(tiled, f32), vm(tiled, f32), vm((3,) + tiled, f32),
         vm(model.shape, f32), vm(tiled, f32), vm(halo, f32), vm(tiled, f32),
         vm(tiled, f32), vm(tiled, f32), vm(tiled, f32), vm(tiled, f32), vm(tiled, f32),
-        vm((4,) + tiled, f32), vm((10, width, nrec), jnp.bfloat16),
+        vm((4,) + tiled, f32), vm((4, width, 3 * nrec), jnp.bfloat16), vm((tiles, depth * tx, nrec), jnp.bfloat16),
         vm(tiled, f32), vm(halo, f32), vm(tiled, f32), vm(halo, f32),
         vm(tiled, f32), vm(part, f32), vm(part, f32), vm(part, f32),
         vm((3, 8, 128), jnp.int32), vm((2, most, 8, 128), f32),
@@ -455,7 +478,7 @@
         out_specs=(vm_spec,) * 3,
         scratch_shapes=scratch,
         compiler_params=pltpu.CompilerParams(
-            collective_id=0, has_side_effects=True, vmem_limit_bytes=56 * 1024 * 1024
+            collective_id=0, has_side_effects=True, vmem_limit_bytes=57 * 1024 * 1024
         ),
     )(intersection, res_data.reshape(3, nrec // 128, 128), rec_index, courant, adj_prev, adj_cur, accel, model)
 

time: 89.5 us -> 82.2 us (0.918)
  Pallas kernels: 84.1 us -> 76.8 us
    pallas_call x1, Pallas kernels: 84.1 us -> 76.8 us  [local(): pl.pallas_call(functools.partial(kernel, dims), out_shape=(pltpu.VMEM(mod...]
where the time goes in v3:
time: 82.2 us; the launch traced here: 81.1 us
  Pallas kernels  76.8 us (93%)
  local copies, waits for them, and re-layouts  3.61 us (4%)
    pallas_call x1, Pallas kernels, local(): pl.pallas_call(functools.partial(kernel, dims), out_shape=(pltpu.VMEM(mod...  76.8 us
    unnamed x3, local copies, waits for them, and re-layouts  3.61 us

profile of v3, /device:TPU:0, one launch (start us, length us, event | category | flops | bytes accessed | tf_op | source)
XLA Modules:
  0.0 81.1 jit_solution(765969102639417677)
XLA Ops:
  0.6 76.8 %shard_map.103 = (f32[8,128,256]{2,1,0:T(8,128)S(1)}, f32[1,8,256,256]{3,2,1,0:T(8,128)S(1)}, f32[1,8,256,256]{3,2,1,0:T(8,128)S(1)}) custom-call(s32[1,8]{1,0:T(1,128)} %inter_ref.1, f32[3,4,128]{2,1,0:T(4,128)} %bitcast.1, s32[1,512]{1,0:T(1,128)} %rec_ref.1, f32[1,8,256,256]{3,2,1,0:T(8,128)} %courant.1, f32[1,8,256,256]{3,2,1,0:T(8,128)} %prev.1, ...), custom_call_target="tpu_custom_call" | custom-call | tf_op jit(solution)/shard_map/pallas_call | solution.py:470
  77.5 1.0 %copy.14 = f32[8,128,256]{2,1,0:T(8,128)} copy(f32[8,128,256]{2,1,0:T(8,128)S(1)} %get-tuple-element.3) | data formatting | bytes 2097152
  78.4 1.3 %copy.15 = f32[1,8,256,256]{3,2,1,0:T(8,128)} copy(f32[1,8,256,256]{3,2,1,0:T(8,128)S(1)} %get-tuple-element.4) | data formatting | bytes 4194304
  79.7 1.3 %copy.16 = f32[1,8,256,256]{3,2,1,0:T(8,128)} copy(f32[1,8,256,256]{3,2,1,0:T(8,128)S(1)} %get-tuple-element.5) | data formatting | bytes 4194304

commit v4 on v3

--- a/solution.py
+++ b/solution.py
@@ -52,14 +52,10 @@
     for dev in greet:
         pl.semaphore_signal(barrier, inc=1, device_id=dev, device_id_type=MESH)
 
-    def strip(j):
-        return slice(j * tx, j * tx + tx)
-
     def load(src, dst, at):
-        copies = [pltpu.make_async_copy(src.at[:, strip(j)], dst.at[j], ld.at[at, j]) for j in range(tiles)]
-        for copy in copies:
-            copy.start()
-        return copies
+        copy = pltpu.make_async_copy(src, dst, ld.at[at])
+        copy.start()
+        return copy
 
     l_cur = load(cur.at[0], ac, 0)
     l_co = load(courant.at[0], co, 1)
@@ -67,12 +63,7 @@
     l_a1 = load(accel.at[0, 1], ax.at[1], 3)
     l_a0 = load(accel.at[0, 0], ax.at[0], 4)
     l_a2 = load(accel.at[0, 2], ax.at[2], 5)
-    l_mo = pltpu.make_async_copy(model, mo, ld.at[6, 0])
-    l_mo.start()
-
-    def wait(copies):
-        for copy in copies:
-            copy.wait()
+    l_mo = load(model, mo, 6)
 
     def remote(src, dst, send, recv, dev):
         return pltpu.make_async_remote_copy(
@@ -126,10 +117,10 @@
 
     pl.semaphore_wait(barrier, len(greet))
 
-    halos_c = []
-    for j in range(tiles):
-        halos_c.append(remote(cur.at[0, depth - 1, strip(j)], ach.at[0, j], h_s.at[0, j], h_r.at[0, j], (z, up)))
-        halos_c.append(remote(cur.at[0, 0, strip(j)], ach.at[1, j], h_s.at[1, j], h_r.at[1, j], (z, down)))
+    halos_c = [
+        remote(cur.at[0, depth - 1], ach.at[0], h_s.at[0], h_r.at[0], (z, up)),
+        remote(cur.at[0, 0], ach.at[1], h_s.at[1], h_r.at[1], (z, down)),
+    ]
     for copy in halos_c:
         copy.start()
     st_a = remote(stv.at[0], stv.at[1], st_s.at[0], st_r.at[0], (pair_a, k))
@@ -150,13 +141,16 @@
         return n - 6.0 * c
 
     def cells(field, halos, d, i, j):
-        c = field[i, d]
-        before = jnp.where(j == 0, 0.0, field[(i + tiles - 1) % tiles, d, tx - 8 : tx])
-        after = jnp.where(j == tiles - 1, 0.0, field[(i + 1) % tiles, d, 0:8])
+        def at(tile, plane):
+            return (plane, tile) if field is ac else (tile, plane)
+
+        c = field[at(i, d)]
+        before = jnp.where(j == 0, 0.0, field[at((i + tiles - 1) % tiles, d) + (slice(tx - 8, tx),)])
+        after = jnp.where(j == tiles - 1, 0.0, field[at((i + 1) % tiles, d) + (slice(0, 8),)])
         edge_low = isinstance(d, int) and d == 0
         edge_high = isinstance(d, int) and d == depth - 1
-        below = jnp.where(k == 0, 0.0, halos[0, i]) if edge_low else field[i, d - 1]
-        above = jnp.where(k == slabs - 1, 0.0, halos[1, i]) if edge_high else field[i, d + 1]
+        below = jnp.where(k == 0, 0.0, halos[0, i]) if edge_low else field[at(i, d - 1)]
+        above = jnp.where(k == slabs - 1, 0.0, halos[1, i]) if edge_high else field[at(i, d + 1)]
         return c, lap(c, below, above, before, after)
 
     def planes(body, first, last):
@@ -171,7 +165,7 @@
 
     def p1_cell(d, j):
         c, l = cells(ac, ach, d, j, j)
-        p1[j, d] = 2.0 * c - ap[j, d] + co[j, d] * l + qd[2, j, d]
+        p1[j, d] = 2.0 * c - ap[d, j] + co[d, j] * l + qd[2, j, d]
 
     def p1_sends(j):
         return (
@@ -179,12 +173,6 @@
             remote(p1.at[j, 0], p1h.at[1, j], p_s.at[1, j], p_r.at[1, j], (z, down)),
         )
 
-    def ad_cell(d, j):
-        c, l = cells(p1, p1h, d, j, j)
-        a = 2.0 * c - ac[j, d] + co[j, d] * l + qd[1, j, d]
-        ad[j, d] = a
-        adj[0, d, pl.ds(pl.multiple_of(j * tx, tx), tx), :] = a
-
     def place(r):
         return (r - start) & (tiles - 1)
 
@@ -200,17 +188,19 @@
         for r in ORDER:
             at = place(r)
             for slot, d in slots[h]:
-                img[r, slot] = ax[1, at, d] * p1[at, d] + ax[0, at, d] * ad[at, d]
+                c, l = cells(p1, p1h, d, at, at)
+                a = 2.0 * c - ac[d, at] + co[d, at] * l + qd[1, at, d]
+                ad[r, d] = a
+                img[r, slot] = ax[1, d, at] * c + ax[0, d, at] * a
             send1(r, h).start()
 
-    wait(l_cur)
-    wait(l_co)
-    wait(l_ap)
+    l_cur.wait()
+    l_co.wait()
+    l_ap.wait()
     planes(p1_cell, 1, depth - 1)
-    planes(ad_cell, 2, depth - 2)
-    wait(l_a1)
-    wait(l_a0)
-    wait(l_a2)
+    l_a1.wait()
+    l_a0.wait()
+    l_a2.wait()
     images(0)
     for copy in halos_c:
         copy.wait_recv()
@@ -223,18 +213,21 @@
         return carry
 
     lax.fori_loop(0, tiles, p1_edge, 0)
-    planes(ad_cell, 1, 2)
-    planes(ad_cell, depth - 2, depth - 1)
-
-    def ad_edge(j, carry):
+
+    def p1_wait(j, carry):
         for copy in p1_sends(j):
             copy.wait_recv()
-        ad_cell(0, j)
-        ad_cell(depth - 1, j)
-        return carry
-
-    lax.fori_loop(0, tiles, ad_edge, 0)
+        return carry
+
+    lax.fori_loop(0, tiles, p1_wait, 0)
     images(1)
+
+    def ad_out(d, carry):
+        for j in range(tiles):
+            adj[0, d, j] = ad[(j + start) & (tiles - 1), d]
+        return carry
+
+    lax.fori_loop(0, depth, ad_out, 0)
 
     receivers((0, 3))
     st_a.wait_recv()
@@ -316,9 +309,9 @@
             send2(r, h).wait_recv()
             at = place(r)
             for slot, d in slots[h]:
-                w = co[at, d] * (part[r, slot] + w2[r, slot])
+                w = co[d, at] * (part[r, slot] + w2[r, slot])
                 wt[r, d] = w
-                b = w * ax[0, at, d]
+                b = w * ax[0, d, at]
                 b1[r, d] = b
                 carry = tally(carry, 0, d, at, b)
             if h == 1:
@@ -332,15 +325,15 @@
     def b2_cell(d, r, carry):
         j = place(r)
         c, l = cells(b1, b1h, d, r, j)
-        b = 2.0 * c + co[j, d] * l + wt[r, d] * ax[1, j, d]
+        b = 2.0 * c + co[d, j] * l + wt[r, d] * ax[1, d, j]
         b2[r, d] = b
         return tally(carry, 1, d, j, b)
 
     def b3_cell(d, j, carry):
         r = (j + start) & (tiles - 1)
         c, l = cells(b2, b2h, d, r, j)
-        b = 2.0 * c - b1[r, d] + co[j, d] * l + wt[r, d] * ax[2, j, d]
-        born[0, d, pl.ds(pl.multiple_of(j * tx, tx), tx), :] = b
+        b = 2.0 * c - b1[r, d] + co[d, j] * l + wt[r, d] * ax[2, d, j]
+        born[0, d, j] = b
         return tally(carry, 2, d, j, b)
 
     def sweep(carry):
@@ -452,27 +445,28 @@
     dma = pltpu.SemaphoreType.DMA
     vm = pltpu.VMEM
     halo = (2, tiles, tx, width)
+    laid = (depth, tiles, tx, width)
     scratch = [
-        vm(tiled, f32), vm(halo, f32), vm(tiled, f32), vm(tiled, f32), vm((3,) + tiled, f32),
+        vm(laid, f32), vm(halo, f32), vm(laid, f32), vm(laid, f32), vm((3,) + laid, f32),
         vm(model.shape, f32), vm(tiled, f32), vm(halo, f32), vm(tiled, f32),
         vm(tiled, f32), vm(tiled, f32), vm(tiled, f32), vm(tiled, f32), vm(tiled, f32),
         vm((4,) + tiled, f32), vm((4, width, 3 * nrec), jnp.bfloat16), vm((tiles, depth * tx, nrec), jnp.bfloat16),
         vm(tiled, f32), vm(halo, f32), vm(tiled, f32), vm(halo, f32),
         vm(tiled, f32), vm(part, f32), vm(part, f32), vm(part, f32),
         vm((3, 8, 128), jnp.int32), vm((2, most, 8, 128), f32),
-        dma((7, tiles)), dma((2, tiles)), dma((2, tiles)), dma((2, tiles)), dma((2, tiles)),
+        dma((7,)), dma((2,)), dma((2,)), dma((2, tiles)), dma((2, tiles)),
         dma((2, 2, tiles)), dma((2, 2, tiles)), dma((2,)), dma((2,)),
         dma((tiles, 2)), dma((tiles, 2)), dma((tiles, 2)), dma((tiles, 2)),
         dma((tiles // 2,)), dma((tiles // 2,)), dma((2, most)), dma((2, most)),
     ]
     any_spec = pl.BlockSpec(memory_space=pl.ANY)
     vm_spec = pl.BlockSpec(memory_space=pltpu.VMEM)
-    return pl.pallas_call(
+    new_model, adj, born = pl.pallas_call(
         functools.partial(kernel, dims),
         out_shape=(
             pltpu.VMEM(model.shape, f32),
-            pltpu.VMEM(courant.shape, f32),
-            pltpu.VMEM(courant.shape, f32),
+            pltpu.VMEM((1,) + laid, f32),
+            pltpu.VMEM((1,) + laid, f32),
         ),
         in_specs=[pl.BlockSpec(memory_space=pltpu.SMEM), vm_spec, vm_spec] + [any_spec] * 5,
         out_specs=(vm_spec,) * 3,
@@ -480,7 +474,11 @@
         compiler_params=pltpu.CompilerParams(
             collective_id=0, has_side_effects=True, vmem_limit_bytes=57 * 1024 * 1024
         ),
-    )(intersection, res_data.reshape(3, nrec // 128, 128), rec_index, courant, adj_prev, adj_cur, accel, model)
+    )(
+        intersection, res_data.reshape(3, nrec // 128, 128), rec_index, courant.reshape((1,) + laid),
+        adj_prev.reshape((1,) + laid), adj_cur.reshape((1,) + laid), accel.reshape((1, 3) + laid), model,
+    )
+    return new_model, adj.reshape(courant.shape), born.reshape(courant.shape)
 
 
 def solution(mesh):

time: 82.2 us -> 80.4 us (0.978)
  Pallas kernels: 76.8 us -> 75 us
    pallas_call x1, Pallas kernels: 76.8 us -> 75 us  [local(): pl.pallas_call(functools.partial(kernel, dims), out_shape=(pltpu.VMEM(mod...]
where the time goes in v4:
time: 80.4 us; the launch traced here: 79.2 us
  Pallas kernels  75 us (93%)
  local copies, waits for them, and re-layouts  3.61 us (4%)
    pallas_call x1, Pallas kernels, local(): pl.pallas_call(functools.partial(kernel, dims), out_shape=(pltpu.VMEM(mod...  75 us
    unnamed x3, local copies, waits for them, and re-layouts  3.61 us

profile of v4, /device:TPU:0, one launch (start us, length us, event | category | flops | bytes accessed | tf_op | source)
XLA Modules:
  0.0 79.2 jit_solution(6353684011441513988)
XLA Ops:
  0.6 75.0 %shard_map.103 = (f32[8,128,256]{2,1,0:T(8,128)S(1)}, f32[1,8,8,32,256]{4,3,2,1,0:T(8,128)S(1)}, f32[1,8,8,32,256]{4,3,2,1,0:T(8,128)S(1)}) custom-call(s32[1,8]{1,0:T(1,128)} %inter_ref.1, f32[3,4,128]{2,1,0:T(4,128)} %bitcast.13, s32[1,512]{1,0:T(1,128)} %rec_ref.1, f32[1,8,8,32,256]{4,3,2,1,0:T(8,128)} %bitcast.10, f32[1,8,8,32,256]{4,3,2,1,0:T(8,128)} %bitcast.11, ...), custom_call_target="tpu_custom_call" | custom-call | tf_op jit(solution)/shard_map/pallas_call | solution.py:464
  75.6 1.0 %copy.14 = f32[8,128,256]{2,1,0:T(8,128)} copy(f32[8,128,256]{2,1,0:T(8,128)S(1)} %get-tuple-element.9) | data formatting | bytes 2097152
  76.6 1.3 %copy.15 = f32[1,8,256,256]{3,2,1,0:T(8,128)} copy(f32[1,8,256,256]{3,2,1,0:T(8,128)S(1)} %bitcast.8) | data formatting | bytes 4194304
  77.9 1.3 %copy.16 = f32[1,8,256,256]{3,2,1,0:T(8,128)} copy(f32[1,8,256,256]{3,2,1,0:T(8,128)S(1)} %bitcast.7) | data formatting | bytes 4194304
